TPU v7x, 32 devices: a whole 2x2x4 slice. The times are simulated.
32 devices in a mesh: dp: 4 (over x, core), vocab: 8 (over z, y).
Axes of the slice: x: 2, y: 2, z: 4, core: 2. Of those that a mesh axis runs over, the one named last changes fastest.
Arguments:
- head_input: bfloat16 [512, 8192], P(('dp', 'vocab')), may hold values from -250 to 250
- body_input: bfloat16 [512, 8192], P(('dp', 'vocab')), may hold values from -6 to 6
- head_weight: bfloat16 [16384, 8192], P('vocab'), may hold values from -0.0625 to 0.0625
- gate_weight: bfloat16 [8192, 14336], P('dp', 'vocab'), may hold values from -0.0625 to 0.0625
- up_weight: bfloat16 [8192, 14336], P('dp', 'vocab'), may hold values from -0.0625 to 0.0625
- down_weight: bfloat16 [8192, 14336], P('dp', 'vocab'), may hold values from -0.046875 to 0.046875
- tile_ids: int32 [1024, 128], P(('dp', 'vocab')), may hold values from 0 to 16383, as said below
- tile_probs: bfloat16 [1024, 128], P(('dp', 'vocab')), may hold values from 0 to 1, as said below
- tile_slot: int32 [512], P('dp'), may hold values from 0 to 255, as said below
Outputs:
- input_grad: bfloat16 [512, 8192], P('dp', 'vocab')
Inputs may be any that keep to these rules, and one draw needn't show every extreme that they name: `tile_ids`: each stored slot lists 128 distinct token ids. `tile_probs`: in every slot the probabilities are positive and sum to at most 0.95. `tile_slot`: A group's store of 256 slots lies on the devices of one index of dp in order of vocab, 32 slots a device; rows of a group use distinct slots, so half of the slots hold no row's tile and are never read; in every group all 32 slots of some device are used, and which device varies.
All inputs are finite; a program needn't handle non-finite values.
Results may differ from a plain program's by a relative error of at most 0.02.
Values may be sent and summed in bfloat16 or wider, within the bound.
A program may use at most 128 MiB of HBM per device.

v0:
```python
import jax
import jax.numpy as jnp
from jax import lax
from jax.sharding import PartitionSpec as P

MICRO = 2
MB_ROWS = 64
LOSS_SCALE = 1024


def merged(shard, axis, combine):
    everything = jax.tree.map(lambda part: lax.all_gather(part, axis), shard)
    leading = jax.tree.map(lambda part: part[0], everything)

    def hop(k, so_far):
        return combine(so_far, jax.tree.map(lambda part: part[k], everything))

    return lax.fori_loop(1, lax.axis_size(axis), hop, leading)


def combine_stats(earlier, later):
    first_max, first_top, first_rest_max, first_rest = earlier
    second_max, second_top, second_rest_max, second_rest = later
    joint_max = jnp.maximum(first_max, second_max)
    joint_top = first_top * jnp.exp(first_max - joint_max) + second_top * jnp.exp(
        second_max - joint_max
    )
    joint_rest_max = jnp.maximum(first_rest_max, second_rest_max)
    joint_rest = first_rest * jnp.exp(first_rest_max - joint_rest_max) + second_rest * jnp.exp(
        second_rest_max - joint_rest_max
    )
    return (joint_max, joint_top, joint_rest_max, joint_rest)


def swiglu_grads(gate_act, up_act, down_grad):
    sigma = jax.nn.sigmoid(gate_act)
    gate_grad = (down_grad * up_act * sigma * (1.0 + gate_act * (1.0 - sigma))).astype(jnp.bfloat16)
    up_grad = (down_grad * gate_act * sigma).astype(jnp.bfloat16)
    return (gate_grad, up_grad)


def body(
    head_input,
    body_input,
    head_weight,
    gate_weight,
    up_weight,
    down_weight,
    tile_ids,
    tile_probs,
    tile_slot,
):
    head_rows, body_rows, store_ids, store_probs = (
        lax.all_gather(head_input, "vocab", axis=0, tiled=True),
        lax.all_gather(body_input, "vocab", axis=0, tiled=True),
        lax.all_gather(tile_ids, "vocab", axis=0, tiled=True),
        lax.all_gather(tile_probs, "vocab", axis=0, tiled=True),
    )
    gate_full, up_full, down_full = (gate_weight, up_weight, down_weight)
    vocab_rows = head_weight.shape[0]
    place = lax.axis_index("vocab")
    shards = lax.axis_size("vocab")
    share = head_rows.shape[1] // shards
    row_ids = store_ids[tile_slot]
    row_probs = store_probs[tile_slot].astype(jnp.float32)
    tail_mass = 1.0 - jnp.sum(row_probs, axis=1, keepdims=True)
    columns = row_ids - place * vocab_rows
    inside = (columns >= 0) & (columns < vocab_rows)
    target = jnp.where(inside, columns, vocab_rows)
    count = row_ids.shape[0]
    lines = jnp.broadcast_to(jnp.arange(count, dtype=jnp.int32)[:, None], row_ids.shape)
    teacher = (
        jnp.zeros((count, vocab_rows), jnp.float32).at[lines, target].add(row_probs, mode="drop")
    )
    chosen = jnp.zeros((count, vocab_rows), jnp.bool_).at[lines, target].set(True, mode="drop")

    def handle(start, length):
        rows_head = head_rows[start : start + length]
        rows_body = body_rows[start : start + length]
        picked = chosen[start : start + length]
        target_probs = teacher[start : start + length]
        tail_part = tail_mass[start : start + length]
        logits = jnp.einsum("rd,vd->rv", rows_head, head_weight, preferred_element_type=jnp.float32)
        local_max = jnp.max(logits, axis=1, keepdims=True)
        rest = jnp.where(picked, -1e30, logits)
        local_rest_max = jnp.max(rest, axis=1, keepdims=True)
        local_top = jnp.sum(
            jnp.where(picked, jnp.exp(logits - local_max), 0.0), axis=1, keepdims=True
        )
        local_rest = jnp.sum(
            jnp.where(picked, 0.0, jnp.exp(rest - local_rest_max)), axis=1, keepdims=True
        )
        row_max, top_sum, rest_max, rest_sum = merged(
            (local_max, local_top, local_rest_max, local_rest), "vocab", combine_stats
        )
        total = top_sum + rest_sum * jnp.exp(rest_max - row_max)
        student = jnp.exp(logits - row_max) / total
        spread = jnp.where(picked, 0.0, jnp.exp(rest - rest_max)) / rest_sum
        top_share = top_sum / total
        logit_grad = (
            LOSS_SCALE
            * (
                student * (1.0 - tail_part)
                + jnp.where(
                    picked, tail_part * student - target_probs, -tail_part * top_share * spread
                )
            )
        ).astype(jnp.bfloat16)
        partial_grad = jnp.dot(logit_grad, head_weight, preferred_element_type=jnp.float32)
        head_full = lax.psum(partial_grad.astype(jnp.bfloat16), "vocab")
        head_own = lax.dynamic_slice_in_dim(head_full, place * share, share, 1)
        body_cols = lax.all_to_all(rows_body, "dp", split_axis=1, concat_axis=0, tiled=True)
        grad_cols = lax.all_to_all(head_full, "dp", split_axis=1, concat_axis=0, tiled=True)
        gate_part = jnp.dot(body_cols, gate_full, preferred_element_type=jnp.float32)
        up_part = jnp.dot(body_cols, up_full, preferred_element_type=jnp.float32)
        down_part = jnp.dot(grad_cols, down_full, preferred_element_type=jnp.float32)
        gate_act, up_act, down_grad = (
            lax.psum_scatter(
                gate_part.astype(jnp.bfloat16), "dp", scatter_dimension=0, tiled=True
            ).astype(jnp.float32),
            lax.psum_scatter(
                up_part.astype(jnp.bfloat16), "dp", scatter_dimension=0, tiled=True
            ).astype(jnp.float32),
            lax.psum_scatter(
                down_part.astype(jnp.bfloat16), "dp", scatter_dimension=0, tiled=True
            ).astype(jnp.float32),
        )
        gate_grad, up_grad = swiglu_grads(gate_act, up_act, down_grad)
        gate_every, up_every = (
            lax.all_gather(gate_grad, "dp", axis=0, tiled=True),
            lax.all_gather(up_grad, "dp", axis=0, tiled=True),
        )
        slice_grad = jnp.einsum(
            "rf,df->rd", gate_every, gate_full, preferred_element_type=jnp.float32
        )
        slice_grad = (
            slice_grad
            + jnp.einsum("rf,df->rd", up_every, up_full, preferred_element_type=jnp.float32)
        ).astype(jnp.bfloat16)
        branch = lax.all_to_all(slice_grad, "dp", split_axis=0, concat_axis=1, tiled=True).astype(
            jnp.float32
        )
        summed = lax.psum_scatter(
            branch.astype(jnp.bfloat16), "vocab", scatter_dimension=1, tiled=True
        ).astype(jnp.float32)
        return (head_own.astype(jnp.float32) + summed).astype(jnp.bfloat16)

    input_grad = jnp.concatenate(
        [handle(index * MB_ROWS, MB_ROWS) for index in range(MICRO)], axis=0
    )
    return input_grad


def solution(mesh):
    return jax.shard_map(
        body,
        mesh=mesh,
        in_specs=(
            P(("dp", "vocab"), None),
            P(("dp", "vocab"), None),
            P("vocab", None),
            P("dp", "vocab"),
            P("dp", "vocab"),
            P("dp", "vocab"),
            P(("dp", "vocab"), None),
            P(("dp", "vocab"), None),
            P("dp"),
        ),
        out_specs=P("dp", "vocab"),
        check_vma=False,
    )
```

profile of v0, /device:TPU:21, one launch (start us, length us, event | category | flops | bytes accessed | tf_op | source)
XLA Modules:
  0.0 755.5 jit_solution(14502667072134060429)
XLA Ops:
  6.5 0.7 all-gather.11.cloned.1.call-update
  7.3 0.7 all-gather.13.cloned.1.call-update
  8.1 0.7 compare_select_fusion.1
  8.7 23.3 %all_gather.54 = bf16[256,128]{1,0:T(8,128)(2,1)S(1)} all-gather(bf16[32,128]{1,0:T(8,128)(2,1)} %param.20), channel_id=1, replica_groups=mesh['dp'=4,'vocab'=8] {'vocab'}, dimensions={0}, use_global_device_ids=true | all-gather | bytes 73728 | tf_op jit(solution)/shard_map/all_gather | solution.py:57
  32.1 0.7 gather_fusion.1
  32.9 25.3 %all_gather.50 = s32[256,128]{1,0:T(8,128)S(1)} all-gather(s32[32,128]{1,0:T(8,128)} %param.19), channel_id=1, replica_groups=mesh['dp'=4,'vocab'=8] {'vocab'}, dimensions={0}, use_global_device_ids=true | all-gather | bytes 147456 | tf_op jit(solution)/shard_map/all_gather | solution.py:56
  58.2 0.6 gather_fusion
  58.9 0.7 multiply_reduce_fusion
  59.7 0.8 and_reduce_fusion
  60.5 68.8 %scatter_custom_fusion = pred[262144]{0:T(1024)(128)(4,1)S(1)} fusion(s32[16384]{0:T(1024)S(1)} %select_bitcast_fusion, pred[16384]{0:T(1024)(128)(4,1)S(1)} %broadcast.131, pred[]{:T(512)} %constant.96.clone.1), kind=kCustom, calls=%fused_computation.68 | custom fusion | bytes 262145
  129.6 86.6 %scatter_custom_fusion.1 = f32[262144]{0:T(1024)S(1)} fusion(s32[16384]{0:T(1024)S(1)} %select_bitcast_fusion, f32[16384]{0:T(1024)S(1)} %convert_bitcast_fusion, f32[]{:T(128)} %constant.101.clone.1), kind=kCustom, calls=%fused_computation.60 | custom fusion | flops 16384 | bytes 1048580
  216.3 0.9 reshape.95
  217.3 0.9 reshape.97
  218.1 0.6 dynamic-slice
  219.4 15.5 %fusion.64 = (f32[64]{0:T(128)S(1)}, f32[64]{0:T(128)S(1)}, f32[64,2048]{1,0:T(8,128)S(1)}) fusion(pred[64,2048]{1,0:T(32,128)(4,1)S(1)} %reshape.94, bf16[2048,8192]{1,0:T(8,128)(2,1)} %param.15, bf16[128,8192]{1,0:T(8,128)(2,1)} %all-gather.11.cloned.1.call-done), kind=kOutput, calls=%fused_computation.109 | convolution fusion | flops 2147876864 | bytes 35258880 | tf_op jit(solution)/shard_map/rd,vd->rv/dot_general | solution.py:83
  234.9 0.4 select_reduce_fusion.2
  235.3 0.2 dynamic-update-slice
  235.7 15.6 %fusion.65 = (f32[64]{0:T(128)S(1)}, f32[64]{0:T(128)S(1)}, f32[64,2048]{1,0:T(8,128)S(1)}) fusion(pred[64,2048]{1,0:T(32,128)(4,1)S(1)} %reshape.96, bf16[2048,8192]{1,0:T(8,128)(2,1)} %param.15, bf16[128,8192]{1,0:T(8,128)(2,1)S(1)} %copy-done), kind=kOutput, calls=%fused_computation.110 | convolution fusion | flops 2147876864 | bytes 35258880 | tf_op jit(solution)/shard_map/rd,vd->rv/dot_general | solution.py:83
  251.3 0.2 dynamic-update-slice.4
  251.6 0.4 select_reduce_fusion
  252.0 0.2 dynamic-update-slice.6
  252.2 0.2 dynamic-update-slice.1
  252.4 0.2 dynamic-update-slice.3
  253.0 25.5 %all-reduce.8 = (f32[512]{0:T(512)S(1)}, f32[512]{0:T(512)S(1)}, f32[512]{0:T(512)S(1)}, f32[512]{0:T(512)S(1)}, f32[512]{0:T(512)S(1)}, /*index=5*/f32[512]{0:T(512)S(1)}, f32[512]{0:T(512)S(1)}, f32[512]{0:T(512)S(1)}) all-reduce(f32[512]{0:T(512)S(1)} %dynamic-update-slice.4, ...), channel_id=6, replica_groups=mesh['dp'=4,'vocab'=8] {'vocab'}, use_global_device_ids=true, to_apply=%add.4 | all-reduce | flops 4096 | bytes 32768
  279.3 0.3 while.42
  279.6 0.3 while.43
  280.0 18.2 %convolution_convert_fusion.1 = bf16[64,8192]{1,0:T(8,128)(2,1)} fusion(bf16[2048,8192]{1,0:T(8,128)(2,1)} %param.15, pred[64,2048]{1,0:T(32,128)(4,1)S(1)} %reshape.94, f32[64,2048]{1,0:T(8,128)} %reshape.95, f32[64,2048]{1,0:T(8,128)S(1)} %get-tuple-element.546, f32[64]{0:T(128)S(1)} %bitcast.192, f32[64]{0:T(128)S(1)} %bitcast.193, ...), kind=kOutput, calls=%fused_computation.33 | convolution fusion | flops 2149842944 | bytes 35784448 | tf_op jit(solution)/shard_map/dot_general | solution.py:109
  298.2 14.9 %convolution_convert_fusion = bf16[64,8192]{1,0:T(8,128)(2,1)} fusion(bf16[2048,8192]{1,0:T(8,128)(2,1)} %param.15, pred[64,2048]{1,0:T(32,128)(4,1)S(1)} %reshape.96, f32[64,2048]{1,0:T(8,128)S(1)} %copy-done.1, f32[64,2048]{1,0:T(8,128)S(1)} %get-tuple-element.545, f32[64]{0:T(128)S(1)} %bitcast.188, f32[64]{0:T(128)S(1)} %bitcast.189, ...), kind=kOutput, calls=%fused_computation.32 | convolution fusion | flops 2149842944 | bytes 35784448 | tf_op jit(solution)/shard_map/dot_general | solution.py:109
  313.2 1.7 fusion.81
  315.0 36.0 %all_to_all.114 = bf16[64,4,2048]{2,0,1:T(8,128)(2,1)S(1)} all-to-all(bf16[64,4,2048]{2,0,1:T(8,128)(2,1)S(1)} %bitcast.172), channel_id=1, replica_groups=mesh['dp'=4,'vocab'=8] {'dp'}, dimensions={1} | all-to-all | bytes 2097152 | tf_op jit(solution)/shard_map/all_to_all | solution.py:112
  351.0 6.1 convolution_convert_fusion.6
  357.1 0.3 reduce-scatter.13.cloned.1.call-start
  357.4 6.1 convolution_convert_fusion.5
  363.6 74.1 %all-reduce.12.cloned.1.call-done = (bf16[64,8192]{1,0:T(8,128)(2,1)}, bf16[64,8192]{1,0:T(8,128)(2,1)}) async-done(((bf16[64,8192]{1,0:T(8,128)(2,1)}, bf16[64,8192]{1,0:T(8,128)(2,1)}), (bf16[64,8192]{1,0:T(8,128)(2,1)}, bf16[64,8192]{1,0:T(8,128)(2,1)})) %all-reduce.12.cloned.1.call-update) | async-done | bytes 2097168 | tf_op jit(solution)/shard_map/psum | solution.py:110
  437.7 1.3 copy.41
  439.0 16.6 %all_to_all.115 = bf16[64,4,2048]{2,0,1:T(8,128)(2,1)S(1)} all-to-all(bf16[64,4,2048]{2,0,1:T(8,128)(2,1)S(1)} %bitcast.175), channel_id=1, replica_groups=mesh['dp'=4,'vocab'=8] {'dp'}, dimensions={1} | all-to-all | bytes 2097152 | tf_op jit(solution)/shard_map/all_to_all | solution.py:113
  455.6 6.3 convolution_convert_fusion.7
  462.1 16.8 %all_to_all.116 = bf16[64,4,2048]{2,0,1:T(8,128)(2,1)S(1)} all-to-all(bf16[64,4,2048]{2,0,1:T(8,128)(2,1)S(1)} %bitcast.173), channel_id=1, replica_groups=mesh['dp'=4,'vocab'=8] {'dp'}, dimensions={1} | all-to-all | bytes 2097152 | tf_op jit(solution)/shard_map/all_to_all | solution.py:112
  478.9 6.1 convolution_convert_fusion.3
  485.1 6.2 convolution_convert_fusion.2
  491.4 16.9 %all_to_all.117 = bf16[64,4,2048]{2,0,1:T(8,128)(2,1)S(1)} all-to-all(bf16[64,4,2048]{2,0,1:T(8,128)(2,1)S(1)} %bitcast.176), channel_id=1, replica_groups=mesh['dp'=4,'vocab'=8] {'dp'}, dimensions={1} | all-to-all | bytes 2097152 | tf_op jit(solution)/shard_map/all_to_all | solution.py:113
  508.3 6.2 convolution_convert_fusion.4
  514.6 2.8 reduce-scatter.9.cloned.1.call-done
  517.4 1.4 fusion.41
  518.8 9.6 %all_gather.56 = bf16[256,1792]{1,0:T(8,128)(2,1)S(1)} all-gather(bf16[64,1792]{1,0:T(8,128)(2,1)S(1)} %get-tuple-element.534), channel_id=1, replica_groups=mesh['dp'=4,'vocab'=8] {'dp'}, dimensions={0}, use_global_device_ids=true | all-gather | bytes 1146880 | tf_op jit(solution)/shard_map/all_gather | solution.py:130
  528.4 9.7 %all_gather.57 = bf16[256,1792]{1,0:T(8,128)(2,1)S(1)} all-gather(bf16[64,1792]{1,0:T(8,128)(2,1)S(1)} %get-tuple-element.533), channel_id=1, replica_groups=mesh['dp'=4,'vocab'=8] {'dp'}, dimensions={0}, use_global_device_ids=true | all-gather | bytes 1146880 | tf_op jit(solution)/shard_map/all_gather | solution.py:131
  538.1 5.3 fusion.84
  543.5 3.1 fusion.20
  546.5 3.6 all-to-all-start.2
  550.2 20.7 %reduce-scatter.21.cloned.1.call-done = bf16[64,1792]{1,0:T(8,128)(2,1)} async-done(((bf16[256,1792]{1,0:T(8,128)(2,1)}), bf16[64,1792]{1,0:T(8,128)(2,1)}) %reduce-scatter.21.cloned.1.call-update) | async-done | bytes 229392 | tf_op jit(solution)/shard_map/reduce_scatter | solution.py:118
  570.9 26.8 %reduce-scatter.17.cloned.1.call-done = bf16[64,1792]{1,0:T(8,128)(2,1)} async-done(((bf16[256,1792]{1,0:T(8,128)(2,1)}), bf16[64,1792]{1,0:T(8,128)(2,1)}) %reduce-scatter.17.cloned.1.call-update) | async-done | bytes 229392 | tf_op jit(solution)/shard_map/reduce_scatter | solution.py:124
  597.7 1.4 fusion.47
  599.1 9.4 %all_gather.62 = bf16[256,1792]{1,0:T(8,128)(2,1)S(1)} all-gather(bf16[64,1792]{1,0:T(8,128)(2,1)S(1)} %get-tuple-element.536), channel_id=1, replica_groups=mesh['dp'=4,'vocab'=8] {'dp'}, dimensions={0}, use_global_device_ids=true | all-gather | bytes 1146880 | tf_op jit(solution)/shard_map/all_gather | solution.py:130
  608.5 9.9 %all_gather.63 = bf16[256,1792]{1,0:T(8,128)(2,1)} all-gather(bf16[64,1792]{1,0:T(8,128)(2,1)S(1)} %get-tuple-element.535), channel_id=1, replica_groups=mesh['dp'=4,'vocab'=8] {'dp'}, dimensions={0}, use_global_device_ids=true | all-gather | bytes 1146880 | tf_op jit(solution)/shard_map/all_gather | solution.py:131
  618.4 1.1 copy.32
  619.6 5.2 fusion.85
  624.8 5.3 fusion.21
  630.1 16.4 %all_to_all.118 = bf16[4,64,2048]{2,1,0:T(8,128)(2,1)S(1)} all-to-all(bf16[4,64,2048]{2,1,0:T(8,128)(2,1)S(1)} %bitcast.185), channel_id=1, replica_groups=mesh['dp'=4,'vocab'=8] {'dp'}, dimensions={0} | all-to-all | bytes 2097152 | tf_op jit(solution)/shard_map/all_to_all | solution.py:140
  646.5 1.1 copy.33
  647.6 33.3 %reduce-scatter.15.cloned.1.call-done = bf16[64,1024]{1,0:T(8,128)(2,1)} async-done(((bf16[64,8192]{1,0:T(8,128)(2,1)}), bf16[64,1024]{1,0:T(8,128)(2,1)}) %reduce-scatter.15.cloned.1.call-update) | async-done | bytes 131088 | tf_op jit(solution)/shard_map/reduce_scatter | solution.py:143
  680.9 1.0 add_convert_fusion.1
  681.9 65.2 %reduce-scatter.23.cloned.1.call-done = bf16[64,1024]{1,0:T(8,128)(2,1)} async-done(((bf16[64,8192]{1,0:T(8,128)(2,1)}), bf16[64,1024]{1,0:T(8,128)(2,1)}) %reduce-scatter.23.cloned.1.call-update) | async-done | bytes 131088 | tf_op jit(solution)/shard_map/reduce_scatter | solution.py:143
  747.0 0.9 add_convert_fusion
  748.0 0.7 pad_maximum_fusion
  (94 shorter events, 3.2 us)
Async XLA Ops:
  6.5 211.6 %copy-start.4 = (u32[32]{0:T(128)S(1)}, u32[32]{0:T(128)}, u32[]{:S(2)}) copy-start(u32[32]{0:T(128)} %constant.126) | copy-start | bytes 388
  6.5 212.9 %all-gather.11.cloned.1.call-start = ((), (), s32[]{:S(2)}) async-start(), calls=%async_computation.14 | async-start | bytes 2359296 | tf_op jit(solution)/shard_map/all_gather | solution.py:54
  7.3 306.0 %all-gather.13.cloned.1.call-start = ((), (), s32[]{:S(2)}) async-start(), calls=%async_computation.16 | async-start | bytes 2359296 | tf_op jit(solution)/shard_map/all_gather | solution.py:55
  8.0 429.7 %all-reduce.12.cloned.1.call-start = ((), (), s32[]{:S(2)}) async-start(), calls=%async_computation.24 | async-start | bytes 4194304 | tf_op jit(solution)/shard_map/psum | solution.py:110
  219.4 16.3 %copy-start = (bf16[128,8192]{1,0:T(8,128)(2,1)S(1)}, bf16[128,8192]{1,0:T(8,128)(2,1)}, u32[]{:S(2)}) copy-start(bf16[128,8192]{1,0:T(8,128)(2,1)} %all-gather.11.cloned.1.call-done) | copy-start | bytes 6291460
  280.0 18.2 %copy-start.1 = (f32[64,2048]{1,0:T(8,128)S(1)}, f32[64,2048]{1,0:T(8,128)}, u32[]{:S(2)}) copy-start(f32[64,2048]{1,0:T(8,128)} %reshape.97) | copy-start | bytes 1572868
  313.1 201.5 %reduce-scatter.11.cloned.1.call-start = ((), (), s32[]{:S(2)}) async-start(), calls=%async_computation.17 | async-start | bytes 1146880 | tf_op jit(solution)/shard_map/reduce_scatter | solution.py:121
  357.1 157.5 %reduce-scatter.13.cloned.1.call-start = ((), (), s32[]{:S(2)}) async-start(), calls=%async_computation.18 | async-start | bytes 1146880 | tf_op jit(solution)/shard_map/reduce_scatter | solution.py:118
  363.5 153.9 %reduce-scatter.9.cloned.1.call-start = ((), (), s32[]{:S(2)}) async-start(), calls=%async_computation.15 | async-start | bytes 1146880 | tf_op jit(solution)/shard_map/reduce_scatter | solution.py:124
  461.9 88.3 %reduce-scatter.19.cloned.1.call-start = ((), (), s32[]{:S(2)}) async-start(), calls=%async_computation.21 | async-start | bytes 1146880 | tf_op jit(solution)/shard_map/reduce_scatter | solution.py:121
  485.0 6.3 copy-start.2
  485.0 85.8 %reduce-scatter.21.cloned.1.call-start = ((), (), s32[]{:S(2)}) async-start(), calls=%async_computation.22 | async-start | bytes 1146880 | tf_op jit(solution)/shard_map/reduce_scatter | solution.py:118
  491.3 106.4 %reduce-scatter.17.cloned.1.call-start = ((), (), s32[]{:S(2)}) async-start(), calls=%async_computation.20 | async-start | bytes 1146880 | tf_op jit(solution)/shard_map/reduce_scatter | solution.py:124
  518.8 24.6 %slice-start = ((s8[7340032]{0:T(1024)(128)(4,1)}), s8[4194304]{0:T(1024)(128)(4,1)S(1)}, s32[]{:S(2)}) async-start(s8[7340032]{0:T(1024)(128)(4,1)} %bitcast.196), calls=%async_computation.25 | async-start | bytes 8388608
  538.1 5.4 slice-start.1
  546.5 71.9 %all-to-all-start.2 = ((bf16[4,64,2048]{2,1,0:T(8,128)(2,1)}), bf16[4,64,2048]{2,1,0:T(8,128)(2,1)S(1)}, u32[]{:S(2)}, u32[]{:S(2)}) async-start(bf16[4,64,2048]{2,1,0:T(8,128)(2,1)} %bitcast.27), calls=%async_computation.5 | async-start | bytes 2097152 | tf_op jit(solution)/shard_map/all_to_all | solution.py:140
  550.2 130.7 %reduce-scatter.15.cloned.1.call-start = ((), (), s32[]{:S(2)}) async-start(), calls=%async_computation.19 | async-start | bytes 1179648 | tf_op jit(solution)/shard_map/reduce_scatter | solution.py:143
  619.5 5.3 copy-start.3
  619.5 127.5 %reduce-scatter.23.cloned.1.call-start = ((), (), s32[]{:S(2)}) async-start(), calls=%async_computation.23 | async-start | bytes 1179648 | tf_op jit(solution)/shard_map/reduce_scatter | solution.py:143
Sparse Core Ops, SparseCore 0:
  9.5 49.6 all-gather.10
  61.3 48.2 all-gather.12
  313.3 124.3 all-reduce.11
  440.1 24.0 reduce-scatter.10
  466.8 24.0 reduce-scatter.12
  493.3 24.0 reduce-scatter.8
  520.1 24.0 reduce-scatter.18
  546.8 24.0 reduce-scatter.20
  573.6 24.0 reduce-scatter.16
  619.6 61.1 reduce-scatter.14
  684.6 62.3 reduce-scatter.22
where the time goes:
time: 766 us; the launch traced here: 756 us
  waiting for transfers between devices  224 us (29%)
  blocking collectives  216 us (28%)
  matrix products  120 us (16%)
  other arithmetic  95.7 us (12%)
  local copies, waits for them, and re-layouts  80.8 us (11%)
  between operations  14.5 us (2%)
    reduce_scatter x2, waiting for transfers between devices, handle(): lax.psum_scatter(branch.astype(jnp.bfloat16), 'vocab', scatter_dimension=...  98.5 us
    unnamed x5, other arithmetic  88.1 us
    psum x1, waiting for transfers between devices, handle(): head_full = lax.psum(partial_grad.astype(jnp.bfloat16), 'vocab')  74.1 us
    unnamed x33, local copies, waits for them, and re-layouts  71.2 us
    all_to_all x2, blocking collectives, handle(): lax.all_to_all(rows_body, 'dp', split_axis=1, concat_axis=0, tiled=True)  52.8 us
    all_to_all x2, blocking collectives, handle(): lax.all_to_all(head_full, 'dp', split_axis=1, concat_axis=0, tiled=True)  33.5 us
    dot_general x2, matrix products, handle(): jnp.dot(logit_grad, head_weight, preferred_element_type=jnp.float32)  33.1 us
    dot_general x2, matrix products, handle(): jnp.einsum('rd,vd->rv', rows_head, head_weight, preferred_element_type=jn...  31.1 us
  transfers between devices with their start and end apart: 12, of which 6 were waited for; matrix products, arithmetic and copies ran while one was open for 39% of the time, Pallas kernels for 0%

commit v1 on v0

v1 whole, which is shorter than its diff:
```python
import functools

import jax
import jax.numpy as jnp
from jax import lax
from jax.experimental import pallas as pl
from jax.experimental.pallas import tpu as pltpu
from jax.sharding import PartitionSpec as P

LOSS_SCALE = 1024
LANES = 128
MESH = pl.DeviceIdType.MESH
VMEM = pltpu.VMEM
F32 = jnp.float32
BF16 = jnp.bfloat16
DMA = pltpu.SemaphoreType.DMA


def params(ident, mib=48):
    return pltpu.CompilerParams(
        collective_id=ident, has_side_effects=True, vmem_limit_bytes=mib * 1024 * 1024
    )


def remote(src, dst, send, recv, where):
    return pltpu.make_async_remote_copy(
        src_ref=src,
        dst_ref=dst,
        send_sem=send,
        recv_sem=recv,
        device_id=where,
        device_id_type=MESH,
    )


def greet(peers):
    barrier = pltpu.get_barrier_semaphore()
    for peer in peers:
        pl.semaphore_signal(barrier, inc=1, device_id=peer, device_id_type=MESH)
    pl.semaphore_wait(barrier, len(peers))


def grid_peers(nv):
    v = lax.axis_index("vocab")
    nz = nv // 2
    z, y = v // 2, lax.rem(v, 2)
    along = [{"vocab": lax.rem(z + s, nz) * 2 + y} for s in range(1, nz)]
    return z, y, along, {"vocab": z * 2 + 1 - y}


def spread_start(nv, source, slot, zs, zr, ys, yr):
    z, y, along, partner = grid_peers(nv)
    mine = z * 2 + y
    copies = []
    for s in range(1, nv // 2):
        copies.append(
            remote(source, slot(mine), zs.at[s - 1], zr.at[s - 1], along[s - 1])
        )
    copies.append(remote(source, slot(mine), ys.at[0], yr.at[0], partner))
    for copy in copies:
        copy.start()
    return copies


def spread_forward(nv, s, slot, zs, zr, ys, yr):
    z, y, along, partner = grid_peers(nv)
    nz = nv // 2
    came = lax.rem(z - s + nz, nz) * 2 + y
    remote(slot(came), slot(came), zs.at[s - 1], zr.at[s - 1], along[s - 1]).wait_recv()
    copy = remote(slot(came), slot(came), ys.at[s], yr.at[s], partner)
    copy.start()
    return copy


def spread_finish(nv, copies, slot, ys, yr):
    z, y, _, partner = grid_peers(nv)
    nz = nv // 2
    for s in range(nz):
        theirs = lax.rem(z - s + nz, nz) * 2 + 1 - y
        remote(slot(theirs), slot(theirs), ys.at[s], yr.at[s], partner).wait_recv()
    for copy in copies:
        copy.wait_send()


def intake_kernel(
    nd, nv, vocab_rows,
    head_ref, body_ref, ids_ref, probs_ref, slot_ref,
    rows_ref, cols_ref, enc_ref, tail_ref,
    ids_all, probs_all, hi_s, lo_s, p_s,
    hzs, hzr, hys, hyr, ts, tr, us, ur, bs, br,
):
    d = lax.axis_index("dp")
    v = lax.axis_index("vocab")
    nz = nv // 2
    z, y, along, partner = grid_peers(nv)
    width = body_ref.shape[1] // nd
    everyone = [{"vocab": lax.rem(v + s, nv)} for s in range(1, nv)]
    others = [{"dp": lax.rem(d + s, nd)} for s in range(1, nd)]
    greet(everyone + others)
    small = []
    for s in range(1, nv):
        small.append(remote(ids_ref, ids_all.at[v], ts.at[s - 1], tr.at[s - 1], everyone[s - 1]))
        small.append(
            remote(probs_ref, probs_all.at[v], us.at[s - 1], ur.at[s - 1], everyone[s - 1])
        )
    for copy in small:
        copy.start()
    heads = spread_start(nv, head_ref, lambda k: rows_ref.at[k], hzs, hzr, hys, hyr)
    crossing = []
    for s in range(1, nd):
        to = lax.rem(d + s, nd)
        part = body_ref.at[:, pl.ds(pl.multiple_of(to * width, width), width)]
        crossing.append(remote(part, cols_ref.at[d], bs.at[s - 1], br.at[s - 1], others[s - 1]))
    for copy in crossing:
        copy.start()
    rows_ref[v] = head_ref[...]
    cols_ref[d] = body_ref[:, pl.ds(pl.multiple_of(d * width, width), width)]
    ids_all[v] = ids_ref[...]
    probs_all[v] = probs_ref[...]
    for s in range(1, nv):
        came = lax.rem(v - s + nv, nv)
        remote(ids_ref, ids_all.at[came], ts.at[s - 1], tr.at[s - 1], everyone[0]).wait_recv()
        remote(probs_ref, probs_all.at[came], us.at[s - 1], ur.at[s - 1], everyone[0]).wait_recv()

    count = slot_ref.shape[0]
    slots = ids_ref.shape[0]
    hi = jnp.zeros((count, LANES), F32)
    lo = jnp.zeros((count, LANES), F32)
    pr = jnp.zeros((count, LANES), F32)
    wanted = slot_ref[...]
    place = lax.broadcasted_iota(jnp.int32, (count, slots), 1)
    for k in range(nv):
        pick = jnp.where(place + k * slots == wanted, 1.0, 0.0).astype(BF16)
        ids = ids_all[k]
        top = lax.shift_right_logical(ids, 7).astype(F32).astype(BF16)
        low = lax.bitwise_and(ids, 127).astype(F32).astype(BF16)
        hi = hi + jnp.dot(pick, top, preferred_element_type=F32)
        lo = lo + jnp.dot(pick, low, preferred_element_type=F32)
        pr = pr + jnp.dot(pick, probs_all[k], preferred_element_type=F32)
    tail_ref[...] = 1.0 - jnp.sum(pr, axis=1, keepdims=True)
    nh = vocab_rows // LANES
    hi_s[...] = hi - (v * nh).astype(F32)
    lo_s[...] = lo
    p_s[...] = pr
    up_high = lax.broadcasted_iota(jnp.int32, (nh, LANES), 0).astype(F32)
    up_low = lax.broadcasted_iota(jnp.int32, (LANES, LANES), 0).astype(F32)

    def eight(step, carry):
        at = pl.multiple_of(step * 8, 8)
        hi8 = hi_s[pl.ds(at, 8), :]
        lo8 = lo_s[pl.ds(at, 8), :]
        p8 = p_s[pl.ds(at, 8), :]
        for j in range(8):
            hot = up_high == hi8[j : j + 1]
            low = jnp.where(up_low == lo8[j : j + 1], 1.0, 0.0).astype(BF16)
            both = jnp.concatenate(
                [jnp.where(hot, p8[j : j + 1], 0.0), jnp.where(hot, 1.0, 0.0)], axis=0
            ).astype(BF16)
            found = lax.dot_general(
                both, low, (((1,), (1,)), ((), ())), preferred_element_type=F32
            )
            enc_ref[at + j] = jnp.where(found[nh:] > 0.5, found[:nh], -1.0)
        return carry

    steps = count // 8
    bounds = [steps * s // nz for s in range(nz + 1)]
    for s in range(nz):
        lax.fori_loop(bounds[s], bounds[s + 1], eight, 0)
        if s + 1 < nz:
            heads.append(
                spread_forward(nv, s + 1, lambda k: rows_ref.at[k], hzs, hzr, hys, hyr)
            )
    spread_finish(nv, heads, lambda k: rows_ref.at[k], hys, hyr)
    for s in range(1, nd):
        came = lax.rem(d - s + nd, nd)
        remote(
            cols_ref.at[came], cols_ref.at[came], bs.at[s - 1], br.at[s - 1], others[0]
        ).wait_recv()
    for copy in crossing + small:
        copy.wait_send()


def intake(nd, nv, vocab_rows, head_input, body_input, ids, probs, slot):
    m, width = head_input.shape
    slots, k = ids.shape
    count = slot.shape[0]
    nz = nv // 2
    return pl.pallas_call(
        functools.partial(intake_kernel, nd, nv, vocab_rows),
        out_shape=(
            jax.ShapeDtypeStruct((nv, m, width), BF16),
            jax.ShapeDtypeStruct((nd, m, width // nd), BF16),
            jax.ShapeDtypeStruct((count, vocab_rows // LANES, LANES), F32),
            jax.ShapeDtypeStruct((count, 1), F32),
        ),
        in_specs=[pl.BlockSpec(memory_space=VMEM)] * 5,
        out_specs=(pl.BlockSpec(memory_space=VMEM),) * 4,
        scratch_shapes=[
            VMEM((nv, slots, k), jnp.int32),
            VMEM((nv, slots, k), BF16),
            VMEM((count, k), F32),
            VMEM((count, k), F32),
            VMEM((count, k), F32),
            DMA((nz,)), DMA((nz,)), DMA((nz,)), DMA((nz,)),
            DMA((nv,)), DMA((nv,)), DMA((nv,)), DMA((nv,)),
            DMA((nd,)), DMA((nd,)),
        ],
        compiler_params=params(0),
    )(head_input, body_input, ids, probs, slot[:, None])


def stats_kernel(nv, logits_ref, enc_ref, tail_ref, grad_ref, mine, got, ss, sr):
    v = lax.axis_index("vocab")
    everyone = [{"vocab": lax.rem(v + s, nv)} for s in range(1, nv)]
    greet(everyone)
    count = logits_ref.shape[0]
    logits = logits_ref[...]
    picked = enc_ref[...] >= 0.0
    top_max = jnp.max(logits, axis=1, keepdims=True)
    rest = jnp.where(picked, -1e30, logits)
    low_max = jnp.max(rest, axis=1, keepdims=True)
    top = jnp.sum(jnp.where(picked, jnp.exp(logits - top_max), 0.0), axis=1, keepdims=True)
    low = jnp.sum(jnp.where(picked, 0.0, jnp.exp(rest - low_max)), axis=1, keepdims=True)
    lane = lax.broadcasted_iota(jnp.int32, (count, LANES), 1)
    packed = jnp.where(
        lane == 0, top_max, jnp.where(lane == 1, top, jnp.where(lane == 2, low_max, low))
    )
    mine[...] = packed.T[0:8]
    got[v] = mine[...]
    copies = [
        remote(mine, got.at[v], ss.at[s - 1], sr.at[s - 1], everyone[s - 1])
        for s in range(1, nv)
    ]
    for copy in copies:
        copy.start()
    for s in range(1, nv):
        came = lax.rem(v - s + nv, nv)
        remote(mine, got.at[came], ss.at[s - 1], sr.at[s - 1], everyone[0]).wait_recv()
    every = [got[k] for k in range(nv)]
    row_max = functools.reduce(jnp.maximum, [e[0:1] for e in every])
    rest_max = functools.reduce(jnp.maximum, [e[2:3] for e in every])
    top_sum = sum(e[1:2] * jnp.exp(e[0:1] - row_max) for e in every)
    rest_sum = sum(e[3:4] * jnp.exp(e[2:3] - rest_max) for e in every)
    total = top_sum + rest_sum * jnp.exp(rest_max - row_max)
    line = lax.broadcasted_iota(jnp.int32, (LANES, count), 0)
    stacked = jnp.where(
        line == 0,
        row_max,
        jnp.where(
            line == 1, 1.0 / total, jnp.where(line == 2, rest_max, top_sum / total / rest_sum)
        ),
    ).T
    tail = tail_ref[...]
    student = jnp.exp(logits_ref[...] - stacked[:, 0:1]) * stacked[:, 1:2]
    kept = enc_ref[...]
    chosen = kept >= 0.0
    spread = jnp.exp(jnp.where(chosen, -1e30, logits_ref[...]) - stacked[:, 2:3])
    grad = student * (1.0 - tail) + jnp.where(
        chosen, tail * student - kept, -(tail * stacked[:, 3:4]) * spread
    )
    grad_ref[...] = (LOSS_SCALE * grad).astype(BF16)
    for copy in copies:
        copy.wait_send()


def logit_gradient(nv, logits, enc, tail):
    count, width = logits.shape
    return pl.pallas_call(
        functools.partial(stats_kernel, nv),
        out_shape=jax.ShapeDtypeStruct((count, width), BF16),
        in_specs=[pl.BlockSpec(memory_space=VMEM)] * 3,
        out_specs=pl.BlockSpec(memory_space=VMEM),
        scratch_shapes=[
            VMEM((8, count), F32),
            VMEM((nv, 8, count), F32),
            DMA((nv,)), DMA((nv,)),
        ],
        compiler_params=params(1),
    )(logits, enc, tail)


def fold(nv, block, total, ybuf, zout, zbuf, ys, yr, zs, zr):
    z, y, along, partner = grid_peers(nv)
    nz = nv // 2
    order = list(range(1, nz)) + [0]
    copies = []
    for s in order:
        target = lax.rem(z + s, nz) * 2 + 1 - y
        copy = remote(block(target), ybuf.at[s], ys.at[s], yr.at[s], partner)
        copy.start()
        copies.append(copy)
    for s in order:
        remote(ybuf.at[s], ybuf.at[s], ys.at[s], yr.at[s], partner).wait_recv()
        own = block(lax.rem(z + s, nz) * 2 + y)[...]
        pair = own.astype(F32) + ybuf[s].astype(F32)
        if s == 0:
            total[...] = pair
        else:
            zout[s - 1] = pair.astype(BF16)
            copy = remote(
                zout.at[s - 1], zbuf.at[s - 1], zs.at[s - 1], zr.at[s - 1], along[s - 1]
            )
            copy.start()
            copies.append(copy)
    for s in range(1, nz):
        remote(
            zout.at[s - 1], zbuf.at[s - 1], zs.at[s - 1], zr.at[s - 1], along[s - 1]
        ).wait_recv()
        total[...] += zbuf[s - 1].astype(F32)
    for copy in copies:
        copy.wait_send()


def swap_pair(nd, nv):
    d = lax.axis_index("dp")
    v = lax.axis_index("vocab")
    c = nv // nd
    pair = {"dp": v // c, "vocab": d * c + lax.rem(v, c)}
    return pair, d != v // c


def swap(nd, nv, source, dest, send, recv):
    pair, other = swap_pair(nd, nv)

    @pl.when(other)
    def _():
        copy = remote(source, dest, send, recv, pair)
        copy.start()
        copy.wait()

    @pl.when(jnp.logical_not(other))
    def _():
        dest[...] = source[...]


def fold_scratch(nv, rows, width):
    nz = nv // 2
    return [
        VMEM((rows, width), F32),
        VMEM((rows, width), BF16),
        VMEM((nz, rows, width), BF16),
        VMEM((nz, rows, width), BF16),
        VMEM((nz, rows, width), BF16),
        DMA((nz,)), DMA((nz,)), DMA((nz,)), DMA((nz,)),
        DMA, DMA,
    ]


def head_kernel(
    nd, nv, part_ref, piece_ref, cols_ref,
    total, held, ybuf, zout, zbuf, ys, yr, zs, zr, ps, pr, gzs, gzr, gys, gyr,
):
    _, _, along, partner = grid_peers(nv)
    v = lax.axis_index("vocab")
    c = nv // nd
    rows, width = piece_ref.shape
    greet(along + [partner, swap_pair(nd, nv)[0]])

    def block(k):
        return part_ref.at[:, pl.ds(pl.multiple_of(k * width, width), width)]

    def slot(k):
        return cols_ref.at[
            pl.ds(pl.multiple_of((k // c) * rows, rows), rows),
            pl.ds(pl.multiple_of(lax.rem(k, c) * width, width), width),
        ]

    fold(nv, block, total, ybuf, zout, zbuf, ys, yr, zs, zr)
    held[...] = total[...].astype(BF16)
    swap(nd, nv, held, piece_ref, ps, pr)
    copies = spread_start(nv, piece_ref, slot, gzs, gzr, gys, gyr)
    slot(v)[...] = piece_ref[...]
    for s in range(1, nv // 2):
        copies.append(spread_forward(nv, s, slot, gzs, gzr, gys, gyr))
    spread_finish(nv, copies, slot, gys, gyr)


def head_exchange(nd, nv, part):
    rows, full = part.shape
    width = full // nv
    nz = nv // 2
    return pl.pallas_call(
        functools.partial(head_kernel, nd, nv),
        out_shape=(
            jax.ShapeDtypeStruct((rows, width), BF16),
            jax.ShapeDtypeStruct((rows * nd, full // nd), BF16),
        ),
        in_specs=[pl.BlockSpec(memory_space=VMEM)],
        out_specs=(pl.BlockSpec(memory_space=VMEM),) * 2,
        scratch_shapes=fold_scratch(nv, rows, width)
        + [DMA((nz,)), DMA((nz,)), DMA((nz,)), DMA((nz,))],
        compiler_params=params(2),
    )(part)


def last_kernel(
    nd, nv, part_ref, piece_ref, out_ref,
    total, held, ybuf, zout, zbuf, ys, yr, zs, zr, ps, pr,
):
    _, _, along, partner = grid_peers(nv)
    c = nv // nd
    rows, width = piece_ref.shape
    greet(along + [partner, swap_pair(nd, nv)[0]])

    def block(k):
        return part_ref.at[
            pl.ds(pl.multiple_of((k // c) * rows, rows), rows),
            pl.ds(pl.multiple_of(lax.rem(k, c) * width, width), width),
        ]

    fold(nv, block, total, ybuf, zout, zbuf, ys, yr, zs, zr)
    held[...] = (total[...] + piece_ref[...].astype(F32)).astype(BF16)
    swap(nd, nv, held, out_ref, ps, pr)


def last_exchange(nd, nv, part, piece):
    rows, width = piece.shape
    return pl.pallas_call(
        functools.partial(last_kernel, nd, nv),
        out_shape=jax.ShapeDtypeStruct((rows, width), BF16),
        in_specs=[pl.BlockSpec(memory_space=VMEM)] * 2,
        out_specs=pl.BlockSpec(memory_space=VMEM),
        scratch_shapes=fold_scratch(nv, rows, width),
        compiler_params=params(3),
    )(part, piece)


CHUNKS = 4


def pair_sum_kernel(nd, part_ref, out_ref, cbuf, xout, xbuf, cs, cr, xs, xr, os, orr):
    d = lax.axis_index("dp")
    nx = nd // 2
    x, core = d // 2, lax.rem(d, 2)
    mate = {"dp": x * 2 + 1 - core}
    far = [{"dp": lax.rem(x + s, nx) * 2 + core} for s in range(1, nx)]
    greet([mate] + far)
    rows = part_ref.shape[0]
    half = rows // 2
    step = half // CHUNKS

    def span(which, k):
        return pl.ds(pl.multiple_of(which * half + k * step, step), step)

    copies = []
    for k in range(CHUNKS):
        copy = remote(part_ref.at[span(1 - core, k)], cbuf.at[k], cs.at[k], cr.at[k], mate)
        copy.start()
        copies.append(copy)
    for k in range(CHUNKS):
        remote(cbuf.at[k], cbuf.at[k], cs.at[k], cr.at[k], mate).wait_recv()
        pair = part_ref[span(core, k), :].astype(F32) + cbuf[k].astype(F32)
        xout[k] = pair.astype(BF16)
        for s in range(1, nx):
            copy = remote(
                xout.at[k], xbuf.at[s - 1, k], xs.at[s - 1, k], xr.at[s - 1, k], far[s - 1]
            )
            copy.start()
            copies.append(copy)
    for k in range(CHUNKS):
        pair = xout[k].astype(F32)
        for s in range(1, nx):
            remote(
                xout.at[k], xbuf.at[s - 1, k], xs.at[s - 1, k], xr.at[s - 1, k], far[s - 1]
            ).wait_recv()
            pair = pair + xbuf[s - 1, k].astype(F32)
        out_ref[span(core, k), :] = pair.astype(BF16)
        place = out_ref.at[span(core, k)]
        copy = remote(place, place, os.at[k], orr.at[k], mate)
        copy.start()
        copies.append(copy)
    for k in range(CHUNKS):
        place = out_ref.at[span(1 - core, k)]
        remote(place, place, os.at[k], orr.at[k], mate).wait_recv()
    for copy in copies:
        copy.wait_send()


def pair_sum(nd, part):
    rows, width = part.shape
    nx = nd // 2
    step = rows // 2 // CHUNKS
    return pl.pallas_call(
        functools.partial(pair_sum_kernel, nd),
        out_shape=jax.ShapeDtypeStruct((rows, width), BF16),
        in_specs=[pl.BlockSpec(memory_space=VMEM)],
        out_specs=pl.BlockSpec(memory_space=VMEM),
        scratch_shapes=[
            VMEM((CHUNKS, step, width), BF16),
            VMEM((CHUNKS, step, width), BF16),
            VMEM((nx - 1, CHUNKS, step, width), BF16),
            DMA((CHUNKS,)), DMA((CHUNKS,)),
            DMA((nx - 1, CHUNKS)), DMA((nx - 1, CHUNKS)),
            DMA((CHUNKS,)), DMA((CHUNKS,)),
        ],
        compiler_params=params(4),
    )(part)


def swiglu_grads(gate_act, up_act, down_grad):
    sigma = jax.nn.sigmoid(gate_act)
    gate_grad = (down_grad * up_act * sigma * (1.0 + gate_act * (1.0 - sigma))).astype(BF16)
    up_grad = (down_grad * gate_act * sigma).astype(BF16)
    return (gate_grad, up_grad)


def body(
    nd, nv,
    head_input, body_input, head_weight, gate_weight, up_weight, down_weight,
    tile_ids, tile_probs, tile_slot,
):
    vocab_rows = head_weight.shape[0]
    count = tile_slot.shape[0]
    m = head_input.shape[0]
    head_rows, cols, enc, tail = intake(
        nd, nv, vocab_rows, head_input, body_input, tile_ids, tile_probs, tile_slot
    )
    every = lax.all_gather(cols, "vocab", axis=0)
    body_cols = every.transpose(1, 0, 2, 3).reshape(nd * nv * m, -1)
    gate_part = jnp.dot(body_cols, gate_weight, preferred_element_type=F32).astype(BF16)
    up_part = jnp.dot(body_cols, up_weight, preferred_element_type=F32).astype(BF16)
    gate_act = lax.psum(gate_part, "dp").astype(F32)
    up_act = lax.psum(up_part, "dp").astype(F32)

    head_rows = head_rows.reshape(count, -1)
    enc = enc.reshape(count, vocab_rows)
    logits = jnp.einsum("rd,vd->rv", head_rows, head_weight, preferred_element_type=F32)
    logit_grad = logit_gradient(nv, logits, enc, tail)
    partial = jnp.dot(logit_grad, head_weight, preferred_element_type=F32).astype(BF16)
    piece, grad_cols = head_exchange(nd, nv, partial)
    down_part = jnp.dot(grad_cols, down_weight, preferred_element_type=F32).astype(BF16)
    down_grad = pair_sum(nd, down_part).astype(F32)
    gate_grad, up_grad = swiglu_grads(gate_act, up_act, down_grad)
    slice_grad = jnp.einsum("rf,df->rd", gate_grad, gate_weight, preferred_element_type=F32)
    slice_grad = (
        slice_grad + jnp.einsum("rf,df->rd", up_grad, up_weight, preferred_element_type=F32)
    ).astype(BF16)
    return last_exchange(nd, nv, slice_grad, piece)


def solution(mesh):
    nd, nv = mesh.shape["dp"], mesh.shape["vocab"]
    return jax.shard_map(
        functools.partial(body, nd, nv),
        mesh=mesh,
        in_specs=(
            P(("dp", "vocab"), None),
            P(("dp", "vocab"), None),
            P("vocab", None),
            P("dp", "vocab"),
            P("dp", "vocab"),
            P("dp", "vocab"),
            P(("dp", "vocab"), None),
            P(("dp", "vocab"), None),
            P("dp"),
        ),
        out_specs=P("dp", "vocab"),
        check_vma=False,
    )
```

time: 766 us -> 323 us (0.42); the launches traced: 756 us -> 323 us
  blocking collectives: 216 us -> 0 us
  Pallas kernels: 0 us -> 206 us
  waiting for transfers between devices: 224 us -> 26.2 us
  other arithmetic: 95.7 us -> 0.01 us
  local copies, waits for them, and re-layouts: 80.8 us -> 7.01 us
  matrix products: 120 us -> 69.4 us
    pallas_call x0 -> x5, Pallas kernels: none -> 206 us  [the longest x1 78.6 us: head_exchange(): pl.pallas_call(functools.partial(head_kernel, nd, nv), out_shape=(jax.Sha...]
    reduce_scatter x8 -> x0, waiting for transfers between devices: 149 us -> none  [the longest x2 98.5 us: handle(): lax.psum_scatter(branch.astype(jnp.bfloat16), 'vocab', scatter_dimension=...]
    all_to_all x5 -> x0, blocking collectives: 103 us -> none  [the longest x2 52.8 us: handle(): lax.all_to_all(rows_body, 'dp', split_axis=1, concat_axis=0, tiled=True)]
    unnamed x5 -> x1, other arithmetic: 88.1 us -> 0.01 us
    all_gather x6 -> x0, blocking collectives: 87.3 us -> none  [the longest x1 25.3 us: body(): lax.all_gather(tile_ids, 'vocab', axis=0, tiled=True)]
    psum x1, waiting for transfers between devices: 74.1 us -> 0.02 us  [body(): gate_act = lax.psum(gate_part, 'dp').astype(F32)]
    unnamed x33 -> x16, local copies, waits for them, and re-layouts: 71.2 us -> 4.37 us
    dot_general x14 -> x7, matrix products: 120 us -> 69.4 us  [the longest x1 15.9 us: body(): jnp.einsum('rd,vd->rv', head_rows, head_weight, preferred_element_type=F32)]
  transfers between devices with their start and end apart: 12 -> 2, of which waited for: 6 -> 1; matrix products, arithmetic and copies ran while one was open for 39% -> 12% of each run, Pallas kernels for 0% -> 38%
where the time goes in v1:
time: 323 us
  Pallas kernels  206 us (64%)
  matrix products  69.4 us (21%)
  waiting for transfers between devices  26.2 us (8%)
  between operations  13.5 us (4%)
  local copies, waits for them, and re-layouts  7.01 us (2%)
    pallas_call x1, Pallas kernels, head_exchange(): pl.pallas_call(functools.partial(head_kernel, nd, nv), out_shape=(jax.Sha...  78.6 us
    pallas_call x1, Pallas kernels, last_exchange(): pl.pallas_call(functools.partial(last_kernel, nd, nv), out_shape=jax.Shap...  52.6 us
    pallas_call x1, Pallas kernels, intake(): pl.pallas_call(functools.partial(intake_kernel, nd, nv, vocab_rows), out_...  29.7 us
    all_gather x1, waiting for transfers between devices, body(): every = lax.all_gather(cols, 'vocab', axis=0)  26.1 us
    pallas_call x1, Pallas kernels, pair_sum(): pl.pallas_call(functools.partial(pair_sum_kernel, nd), out_shape=jax.Shap...  25.4 us
    pallas_call x1, Pallas kernels, logit_gradient(): pl.pallas_call(functools.partial(stats_kernel, nv), out_shape=jax.ShapeDt...  20.1 us
    dot_general x1, matrix products, body(): jnp.einsum('rd,vd->rv', head_rows, head_weight, preferred_element_type=F32)  15.9 us
    dot_general x1, matrix products, body(): jnp.dot(logit_grad, head_weight, preferred_element_type=F32).astype(BF16)  15.7 us
  transfers between devices with their start and end apart: 2, of which 1 were waited for; matrix products, arithmetic and copies ran while one was open for 12% of the time, Pallas kernels for 38%

profile of v1, /device:TPU:21, one launch (start us, length us, event | category | flops | bytes accessed | tf_op | source)
XLA Modules:
  0.0 322.5 jit_solution(10153059876433115214)
XLA Ops:
  6.5 0.0 all-gather.3.cloned.1.call-start
  6.5 0.8 copy.14.slot_ref
  7.3 0.0 copy-start
  7.3 0.9 copy-done
  8.2 0.0 copy-start.1
  8.3 0.9 copy-done.1
  9.2 0.0 copy-start.2
  9.2 0.7 copy-done.2
  9.9 0.0 copy-start.3
  9.9 0.7 copy-done.3
  10.6 29.7 %shard_map.91 = (bf16[8,16,8192]{2,1,0:T(8,128)(2,1)S(1)}, bf16[4,16,2048]{2,1,0:T(8,128)(2,1)}, f32[128,16,128]{2,1,0:T(8,128)S(1)}, f32[128,1]{1,0:T(8,128)S(1)}) custom-call(bf16[16,8192]{1,0:T(8,128)(2,1)S(1)} %copy-done, bf16[16,8192]{1,0:T(8,128)(2,1)S(1)} %copy-done.1, s32[32,128]{1,0:T(8,128)S(1)} %copy-done.2, bf16[32,128]{1,0:T(8,128)(2,1)S(1)} %copy-done.3, ...), custom_call_target="tpu_custom_call" | custom-call | tf_op jit(solution)/shard_map/pallas_call | solution.py:188
  40.3 0.0 all-gather.3.cloned.1.call-update
  40.3 0.0 all-reduce.3.cloned.1.call-start
  40.4 0.3 copy.18
  40.7 15.9 %fusion.16.logits_ref = f32[128,2048]{1,0:T(8,128)S(1)} fusion(bf16[128,8192]{1,0:T(8,128)(2,1)S(1)} %bitcast.23, bf16[2048,8192]{1,0:T(8,128)(2,1)} %param.11), kind=kOutput, calls=%fused_computation.24 | convolution fusion | flops 4294967296 | bytes 36700160 | tf_op jit(solution)/shard_map/rd,vd->rv/dot_general | solution.py:527
  56.6 20.1 %shard_map.92 = bf16[128,2048]{1,0:T(8,128)(2,1)S(1)} custom-call(f32[128,2048]{1,0:T(8,128)S(1)} %fusion.16.logits_ref, f32[128,2048]{1,0:T(8,128)S(1)} %bitcast.22, f32[128,1]{1,0:T(8,128)S(1)} %get-tuple-element.13.tail_ref), custom_call_target="tpu_custom_call" | custom-call | tf_op jit(solution)/shard_map/pallas_call | solution.py:268
  76.7 26.1 %all-gather.3.cloned.1.call-done = bf16[32,16,2048]{2,1,0:T(8,128)(2,1)} async-done(((bf16[4,16,2048]{2,1,0:T(8,128)(2,1)}), bf16[32,16,2048]{2,1,0:T(8,128)(2,1)}) %all-gather.3.cloned.1.call-update) | async-done | bytes 2097168 | tf_op jit(solution)/shard_map/all_gather | solution.py:518
  102.9 0.0 slice-start
  102.9 1.9 copy.15
  104.8 0.0 slice-start.1
  104.8 8.4 %convolution_convert_fusion.1 = bf16[512,1792]{1,0:T(8,128)(2,1)} fusion(bf16[512,2048]{1,0:T(8,128)(2,1)S(1)} %bitcast.26, bf16[2048,1792]{1,0:T(8,128)(2,1)} %param.12), kind=kOutput, calls=%fused_computation.15 | convolution fusion | flops 3759013888 | bytes 11272192 | tf_op jit(solution)/shard_map/dot_general | solution.py:520
  113.2 0.0 slice-done
  113.2 0.0 slice-done.1
  113.2 5.1 %convolution_convert_fusion.2 = bf16[512,1792]{1,0:T(8,128)(2,1)} fusion(bf16[512,2048]{1,0:T(8,128)(2,1)S(1)} %bitcast.27, bf16[2048,1792]{1,0:T(8,128)(2,1)S(1)} %bitcast.30), kind=kOutput, calls=%fused_computation.16 | convolution fusion | flops 3759013888 | bytes 11272192 | tf_op jit(solution)/shard_map/dot_general | solution.py:521
  118.3 0.0 all-reduce.3.cloned.1.call-update
  118.3 15.7 %convolution_convert_fusion.part_ref = bf16[128,8192]{1,0:T(8,128)(2,1)S(1)} fusion(bf16[128,2048]{1,0:T(8,128)(2,1)S(1)} %shard_map.92, bf16[2048,8192]{1,0:T(8,128)(2,1)} %param.11), kind=kOutput, calls=%fused_computation | convolution fusion | flops 4296015872 | bytes 36175872 | tf_op jit(solution)/shard_map/dot_general | solution.py:529
  134.0 78.6 %shard_map.93 = (bf16[128,1024]{1,0:T(8,128)(2,1)S(1)}, bf16[512,2048]{1,0:T(8,128)(2,1)S(1)}) custom-call(bf16[128,8192]{1,0:T(8,128)(2,1)S(1)} %convolution_convert_fusion.part_ref), custom_call_target="tpu_custom_call" | custom-call | tf_op jit(solution)/shard_map/pallas_call | solution.py:382
  212.6 7.1 %convolution_convert_fusion.3.part_ref = bf16[512,1792]{1,0:T(8,128)(2,1)S(1)} fusion(bf16[512,2048]{1,0:T(8,128)(2,1)S(1)} %get-tuple-element.14, bf16[2048,1792]{1,0:T(8,128)(2,1)} %param.14), kind=kOutput, calls=%fused_computation.17 | convolution fusion | flops 3759013888 | bytes 11272192 | tf_op jit(solution)/shard_map/dot_general | solution.py:531
  219.7 25.4 %shard_map.94 = bf16[512,1792]{1,0:T(8,128)(2,1)S(1)} custom-call(bf16[512,1792]{1,0:T(8,128)(2,1)S(1)} %convolution_convert_fusion.3.part_ref), custom_call_target="tpu_custom_call" | custom-call | tf_op jit(solution)/shard_map/pallas_call | solution.py:483
  245.0 0.0 all-reduce.3.cloned.1.call-done
  245.1 0.0 copy-start.4
  245.1 9.7 %fusion.10 = f32[512,2048]{1,0:T(8,128)S(1)} fusion(bf16[2048,1792]{1,0:T(8,128)(2,1)} %param.12, bf16[512,1792]{1,0:T(8,128)(2,1)S(1)} %shard_map.94, bf16[512,1792]{1,0:T(8,128)(2,1)} %get-tuple-element.17, bf16[512,1792]{1,0:T(8,128)(2,1)} %get-tuple-element.18), kind=kOutput, calls=%fused_computation.18 | convolution fusion | flops 3770023936 | bytes 17039360 | tf_op jit(solution)/shard_map/rf,df->rd/dot_general | solution.py:534
  254.8 0.0 copy-done.4
  254.8 7.5 %add_convert_fusion.part_ref = bf16[512,2048]{1,0:T(8,128)(2,1)S(1)} fusion(f32[512,2048]{1,0:T(8,128)S(1)} %fusion.10, bf16[2048,1792]{1,0:T(8,128)(2,1)} %param.13, bf16[512,1792]{1,0:T(8,128)(2,1)S(1)} %copy-done.4, bf16[512,1792]{1,0:T(8,128)(2,1)S(1)} %shard_map.94), kind=kOutput, calls=%fused_computation.5 | convolution fusion | flops 3767533568 | bytes 17301504 | tf_op jit(solution)/shard_map/rf,df->rd/dot_general | solution.py:536
  262.3 52.6 %shard_map.95 = bf16[128,1024]{1,0:T(8,128)(2,1)S(1)} custom-call(bf16[512,2048]{1,0:T(8,128)(2,1)S(1)} %add_convert_fusion.part_ref, bf16[128,1024]{1,0:T(8,128)(2,1)S(1)} %get-tuple-element.16.piece_ref), custom_call_target="tpu_custom_call" | custom-call | tf_op jit(solution)/shard_map/pallas_call | solution.py:418
  315.0 0.7 copy.22
  (1 shorter events, 0.0 us)
Async XLA Ops:
  6.5 96.3 %all-gather.3.cloned.1.call-start = ((), (), s32[]{:S(2)}) async-start(), calls=%async_computation | async-start | bytes 2359296 | tf_op jit(solution)/shard_map/all_gather | solution.py:518
  7.3 0.9 copy-start
  8.2 0.9 copy-start.1
  9.2 0.7 copy-start.2
  9.9 0.7 copy-start.3
  40.3 204.7 %all-reduce.3.cloned.1.call-start = ((), (), s32[]{:S(2)}) async-start(), calls=%async_computation.1 | async-start | bytes 7340032 | tf_op jit(solution)/shard_map/psum | solution.py:522
  102.9 10.3 %slice-start = ((s8[7340032]{0:T(1024)(128)(4,1)}), s8[4194304]{0:T(1024)(128)(4,1)S(1)}, s32[]{:S(2)}) async-start(s8[7340032]{0:T(1024)(128)(4,1)} %bitcast.29), calls=%async_computation.2 | async-start | bytes 8388608
  104.8 8.4 %slice-start.1 = ((s8[7340032]{0:T(1024)(128)(4,1)}), s8[3145728]{0:T(1024)(128)(4,1)S(1)}, s32[]{:S(2)}) async-start(s8[7340032]{0:T(1024)(128)(4,1)} %bitcast.29), calls=%async_computation.3 | async-start | bytes 6291456
  245.1 9.8 %copy-start.4 = (bf16[512,1792]{1,0:T(8,128)(2,1)S(1)}, bf16[512,1792]{1,0:T(8,128)(2,1)}, u32[]{:S(2)}) copy-start(bf16[512,1792]{1,0:T(8,128)(2,1)} %get-tuple-element.17) | copy-start | bytes 5505028
Sparse Core Ops, SparseCore 0:
  40.5 62.3 all-gather.2
  118.4 83.1 all-reduce.2
